TPU v7x, 256 devices: a whole 4x4x8 slice. The times are simulated.
256 devices in a mesh: wide: 32 (over y_lo, z, core), narrow: 8 (over y_hi, x).
Axes of the slice: x: 4, y: 4 (y_hi: 2, y_lo: 2; y = y_hi * 2 + y_lo), z: 8, core: 2. Of those that a mesh axis runs over, the one named last changes fastest.
Arguments:
- velocity: float32 [3, 256, 256, 512], P(None, 'narrow', 'wide'), may hold values from -6 to 6
- slope_x: float32 [512, 512], replicated, may hold values from -0.25 to 0.25
- curve_x: float32 [512, 512], replicated, may hold values from -0.25 to 0.25
- slope_y: float32 [256, 256], replicated, may hold values from -0.375 to 0.375
- curve_y: float32 [256, 256], replicated, may hold values from -0.375 to 0.375
- slope_z: float32 [256, 256], replicated, may hold values from -0.375 to 0.375
- curve_z: float32 [256, 256], replicated, may hold values from -0.375 to 0.375
Outputs:
- forcing: float32 [3, 256, 256, 512], P(None, 'narrow', 'wide')
All inputs are finite; a program needn't handle non-finite values.
Results may differ from a plain program's by a relative error of at most 0.0001.
Values sent between devices are 32-bit elements; how exact they have to be, the bound alone decides.
A program may use at most 128 MiB of HBM per device.

v0:
```python
import jax
import jax.numpy as jnp
from jax import lax
from jax.sharding import PartitionSpec as P

viscosity = 0.5


def contribution(fields, products, slopes, curves, direction, formula):
    pair = jnp.concatenate([products, fields], axis=0)
    derived = jnp.einsum(formula, slopes, pair, precision=lax.Precision.HIGHEST)
    second_order = jnp.einsum(formula, curves, fields, precision=lax.Precision.HIGHEST)
    return -0.5 * (derived[:3] + fields[direction] * derived[3:]) + viscosity * second_order


def on_device(velocity, slope_x, curve_x, slope_y, curve_y, slope_z, curve_z):
    part_x = contribution(velocity, velocity * velocity[0], slope_x, curve_x, 0, "xk,cyzk->cyzx")
    extras = jnp.stack(
        [
            velocity[0] * velocity[1],
            velocity[1] * velocity[1],
            velocity[1] * velocity[2],
            velocity[0] * velocity[2],
            velocity[2] * velocity[2],
        ]
    )
    bundle = jnp.concatenate([velocity, extras], axis=0)
    gathered_y = lax.all_to_all(bundle, "narrow", split_axis=3, concat_axis=1, tiled=True)
    fields_y = gathered_y[:3]
    part_y = contribution(fields_y, gathered_y[3:6], slope_y, curve_y, 1, "yk,ckzx->cyzx")
    onward = jnp.concatenate([fields_y, gathered_y[6:7], gathered_y[5:6], gathered_y[7:8]], axis=0)
    gathered_z = lax.all_to_all(onward, "wide", split_axis=1, concat_axis=2, tiled=True)
    part_z = contribution(gathered_z[:3], gathered_z[3:], slope_z, curve_z, 2, "zk,cykx->cyzx")
    returned = lax.all_to_all(part_z, "wide", split_axis=2, concat_axis=1, tiled=True) + part_y
    return lax.all_to_all(returned, "narrow", split_axis=1, concat_axis=3, tiled=True) + part_x


def solution(mesh):
    return jax.shard_map(
        on_device,
        mesh=mesh,
        in_specs=(P(None, "narrow", "wide", None), P(), P(), P(), P(), P(), P()),
        out_specs=P(None, "narrow", "wide", None),
        check_vma=False,
    )
```

profile of v0, /device:TPU:1, one launch (start us, length us, event | category | flops | bytes accessed | tf_op | source)
XLA Modules:
  0.0 422.7 jit_solution(2023913589087142504)
XLA Ops:
  1.2 3.6 broadcast_multiply_fusion
  9.1 14.6 %copy.55 = f32[8,32,8,512]{1,2,0,3:T(8,128)} copy(f32[8,32,8,512]{3,2,1,0:T(8,128)} %multiply_dynamic-update-slice_fusion) | data formatting | bytes 8388608 | tf_op jit(solution)/shard_map/concatenate | solution.py:27
  23.7 12.9 %reshape.17 = f32[8,1,131072]{2,1,0:T(1,128)} reshape(f32[512,8,8,32]{3,2,1,0:T(8,128)} %bitcast.78) | data formatting | bytes 8388608
  36.5 57.8 %all_to_all.66 = f32[8,1,131072]{2,1,0:T(1,128)} all-to-all(f32[8,1,131072]{2,1,0:T(1,128)} %reshape.17), channel_id=1, replica_groups=mesh['wide'=32,'narrow'=8] {'narrow'}, dimensions={0} | all-to-all | bytes 8388608 | tf_op jit(solution)/shard_map/all_to_all | solution.py:28
  94.9 13.7 %reduce = f32[8,131072]{1,0:T(8,128)} reduce(f32[8,1,131072]{2,1,0:T(1,128)} %all_to_all.66, f32[]{:T(128)} %broadcast.4), dimensions={1}, to_apply=%all_to_all.48.reduce_sub_computation | reduce | bytes 8388612 | tf_op jit(solution)/shard_map/all_to_all | solution.py:28
  108.6 13.4 %reshape.18 = f32[512,8,8,32]{3,2,1,0:T(8,128)} reshape(f32[8,131072]{1,0:T(8,128)} %reduce) | data formatting | bytes 8388608
  122.0 12.8 %copy.56 = f32[8,32,8,8,64]{4,2,1,3,0:T(8,128)} copy(f32[8,32,8,8,64]{1,2,0,4,3:T(8,128)} %bitcast.79) | data formatting | bytes 8388608 | tf_op jit(solution)/shard_map/all_to_all | solution.py:28
  134.7 3.6 fusion.38
  146.5 7.4 %reshape.19 = f32[32,1,24576]{2,1,0:T(1,128)} reshape(f32[256,6,8,64]{3,2,1,0:T(8,128)} %copy_bitcast_fusion.4) | data formatting | bytes 6291456
  153.8 82.5 %all_to_all.67 = f32[32,1,24576]{2,1,0:T(1,128)} all-to-all(f32[32,1,24576]{2,1,0:T(1,128)} %reshape.19), channel_id=1, replica_groups=mesh['wide'=32,'narrow'=8] {'wide'}, dimensions={0} | all-to-all | bytes 6291456 | tf_op jit(solution)/shard_map/all_to_all | solution.py:32
  236.3 12.0 %reduce.1 = f32[32,24576]{1,0:T(8,128)} reduce(f32[32,1,24576]{2,1,0:T(1,128)} %all_to_all.67, f32[]{:T(128)} %broadcast.4), dimensions={1}, to_apply=%all_to_all.51.reduce_sub_computation | reduce | bytes 6291460 | tf_op jit(solution)/shard_map/all_to_all | solution.py:32
  248.4 6.1 %reshape.20 = f32[256,6,8,64]{3,2,1,0:T(8,128)} reshape(f32[32,24576]{1,0:T(8,128)} %reduce.1) | data formatting | bytes 6291456
  259.9 3.4 copy_bitcast_fusion
  272.2 5.4 %fusion.15 = f32[6,8,256,64]{2,3,1,0:T(8,128)S(1)} fusion(f32[3,8,256,64]{2,3,1,0:T(8,128)} %copy.62, f32[3,8,256,64]{2,3,1,0:T(8,128)} %copy.61, f32[256,256]{1,0:T(8,128)S(1)} %copy-done.9), kind=kOutput, calls=%fused_computation.16 | convolution fusion | flops 2416705536 | bytes 6553600 | tf_op jit(solution)/shard_map/zk,cykx->cyzx/dot_general | solution.py:11
  277.6 6.4 %fusion.28 = f32[3,8,256,64]{2,3,1,0:T(8,128)} fusion(f32[6,8,256,64]{2,3,1,0:T(8,128)S(1)} %fusion.15, f32[8,256,64]{1,2,0:T(8,128)S(1)} %copy-done.6, f32[256,256]{1,0:T(8,128)S(1)} %copy-done.7, f32[3,8,32,8,64]{4,3,1,2,0:T(8,128)S(1)} %copy-done.4), kind=kOutput, calls=%fused_computation.30 | convolution fusion | flops 1209925632 | bytes 7077888 | tf_op jit(solution)/shard_map/zk,cykx->cyzx/dot_general | solution.py:12
  287.3 4.4 %reshape.21 = f32[32,1,12288]{2,1,0:T(1,128)} reshape(f32[256,3,8,64]{3,2,1,0:T(8,128)} %bitcast.87) | data formatting | bytes 3145728
  291.7 6.8 %all-to-all-start.2 = ((f32[32,1,12288]{2,1,0:T(1,128)}), f32[32,1,12288]{2,1,0:T(1,128)}, u32[]{:S(2)}, u32[]{:S(2)}) async-start(f32[32,1,12288]{2,1,0:T(1,128)} %reshape.21), calls=%async_computation.2 | async-start | bytes 3145728 | tf_op jit(solution)/shard_map/all_to_all | solution.py:34
  307.4 6.2 %fusion.12 = f32[6,256,8,64]{1,3,2,0:T(8,128)} fusion(f32[3,256,8,64]{1,3,2,0:T(8,128)} %copy.70, f32[3,256,8,64]{1,3,2,0:T(8,128)} %copy.69, f32[256,256]{1,0:T(8,128)S(1)} %copy-done.10), kind=kOutput, calls=%fused_computation.15 | convolution fusion | flops 2416705536 | bytes 6553600 | tf_op jit(solution)/shard_map/yk,ckzx->cyzx/dot_general | solution.py:11
  313.6 23.2 %all-to-all-done.2 = f32[32,1,12288]{2,1,0:T(1,128)} async-done(((f32[32,1,12288]{2,1,0:T(1,128)}), f32[32,1,12288]{2,1,0:T(1,128)}, u32[]{:S(2)}, u32[]{:S(2)}) %all-to-all-start.2) | async-done | bytes 1572896 | tf_op jit(solution)/shard_map/all_to_all | solution.py:34
  336.8 7.0 %reduce.2 = f32[32,12288]{1,0:T(8,128)} reduce(f32[32,1,12288]{2,1,0:T(1,128)} %all-to-all-done.2, f32[]{:T(128)} %broadcast.4), dimensions={1}, to_apply=%all_to_all.54.reduce_sub_computation | reduce | bytes 3145732 | tf_op jit(solution)/shard_map/all_to_all | solution.py:34
  343.8 3.6 reshape.22
  347.4 4.3 %copy.68 = f32[3,32,8,8,64]{4,3,2,1,0:T(8,128)} copy(f32[3,32,8,8,64]{4,2,0,3,1:T(8,128)} %bitcast.88) | data formatting | bytes 3145728 | tf_op jit(solution)/shard_map/all_to_all | solution.py:34
  355.0 5.6 %fusion.25 = f32[3,256,8,64]{1,3,2,0:T(8,128)} fusion(f32[3,256,8,64]{1,3,2,0:T(8,128)} %copy.73, f32[6,256,8,64]{1,3,2,0:T(8,128)} %fusion.12, f32[3,256,8,64]{1,3,2,0:T(8,128)} %copy.70, f32[256,8,64]{0,2,1:T(8,128)} %copy.71, f32[256,256]{1,0:T(8,128)S(1)} %copy-done.8), kind=kOutput, calls=%fused_computation.26 | convolution fusion | flops 1210318848 | bytes 8650752 | tf_op jit(solution)/shard_map/yk,ckzx->cyzx/dot_general | solution.py:12
  363.9 5.0 %reshape.23 = f32[8,1,49152]{2,1,0:T(1,128)} reshape(f32[256,3,8,64]{3,2,1,0:T(8,128)} %bitcast.90) | data formatting | bytes 3145728
  368.9 4.3 %all-to-all-start.3 = ((f32[8,1,49152]{2,1,0:T(1,128)}), f32[8,1,49152]{2,1,0:T(1,128)}, u32[]{:S(2)}, u32[]{:S(2)}) async-start(f32[8,1,49152]{2,1,0:T(1,128)} %reshape.23), calls=%async_computation.3 | async-start | bytes 3145728 | tf_op jit(solution)/shard_map/all_to_all | solution.py:35
  373.2 7.7 %fusion.8 = f32[6,32,8,512]{3,2,1,0:T(8,128)} fusion(f32[3,32,8,512]{3,2,1,0:T(8,128)S(1)} %copy-done.1, f32[3,32,8,512]{3,2,1,0:T(8,128)} %get-tuple-element.13, f32[512,512]{1,0:T(8,128)S(1)} %copy-done), kind=kOutput, calls=%fused_computation.9 | convolution fusion | flops 4832624640 | bytes 7340032 | tf_op jit(solution)/shard_map/xk,cyzk->cyzx/dot_general | solution.py:11
  380.9 15.3 %all-to-all-done.3 = f32[8,1,49152]{2,1,0:T(1,128)} async-done(((f32[8,1,49152]{2,1,0:T(1,128)}), f32[8,1,49152]{2,1,0:T(1,128)}, u32[]{:S(2)}, u32[]{:S(2)}) %all-to-all-start.3) | async-done | bytes 1572896 | tf_op jit(solution)/shard_map/all_to_all | solution.py:35
  396.1 7.0 %reduce.3 = f32[8,49152]{1,0:T(8,128)} reduce(f32[8,1,49152]{2,1,0:T(1,128)} %all-to-all-done.3, f32[]{:T(128)} %broadcast.4), dimensions={1}, to_apply=%all_to_all.58.reduce_sub_computation | reduce | bytes 3145732 | tf_op jit(solution)/shard_map/all_to_all | solution.py:35
  403.1 4.4 %reshape.24 = f32[256,3,8,64]{3,2,1,0:T(8,128)} reshape(f32[8,49152]{1,0:T(8,128)} %reduce.3) | data formatting | bytes 3145728
  407.4 5.4 %copy.76 = f32[3,32,8,8,64]{4,3,2,1,0:T(8,128)} copy(f32[3,32,8,8,64]{4,2,0,1,3:T(8,128)} %bitcast.91) | data formatting | bytes 3145728 | tf_op jit(solution)/shard_map/all_to_all | solution.py:35
  412.9 3.7 all_to_all.61
  416.6 5.9 %fusion.21 = f32[3,32,8,512]{3,2,1,0:T(8,128)} fusion(f32[3,32,8,512]{3,2,1,0:T(8,128)} %all_to_all.61, f32[6,32,8,512]{3,2,1,0:T(8,128)} %fusion.8, f32[3,32,8,512]{3,2,1,0:T(8,128)S(1)} %copy-done.1, f32[512,512]{1,0:T(8,128)} %param.9, f32[32,8,512]{2,1,0:T(8,128)S(1)} %slice_bitcast_fusion), kind=kOutput, calls=%fused_computation.21 | convolution fusion | flops 2418278400 | bytes 9437184 | tf_op jit(solution)/shard_map/xk,cyzk->cyzx/dot_general | solution.py:12
  (43 shorter events, 47.4 us)
Async XLA Ops:
  0.0 373.2 %copy-start = (f32[512,512]{1,0:T(8,128)S(1)}, f32[512,512]{1,0:T(8,128)}, u32[]{:S(2)}) copy-start(f32[512,512]{1,0:T(8,128)} %param.8) | copy-start | bytes 3145732
  0.0 4.8 %copy-start.1 = (f32[3,32,8,512]{3,2,1,0:T(8,128)S(1)}, f32[3,32,8,512]{3,2,1,0:T(8,128)}, u32[]{:S(2)}) copy-start(f32[3,32,8,512]{3,2,1,0:T(8,128)} %param.7) | copy-start | bytes 4718596
  134.7 5.0 %copy-start.2 = (f32[8,32,8,8,64]{4,2,1,3,0:T(8,128)S(1)}, f32[8,32,8,8,64]{4,2,1,3,0:T(8,128)}, u32[]{:S(2)}) copy-start(f32[8,32,8,8,64]{4,2,1,3,0:T(8,128)} %copy.56) | copy-start | bytes 12582916
  141.9 1.7 copy-start.5
  258.7 4.5 %copy-start.3 = (f32[3,8,32,8,64]{4,3,1,2,0:T(8,128)}, f32[3,8,32,8,64]{4,3,1,2,0:T(8,128)S(1)}, u32[]{:S(2)}) copy-start(f32[3,8,32,8,64]{4,3,1,2,0:T(8,128)S(1)} %get-tuple-element.12) | copy-start | bytes 4718596
  266.5 5.6 %copy-start.9 = (f32[256,256]{1,0:T(8,128)S(1)}, f32[256,256]{1,0:T(8,128)}, u32[]{:S(2)}) copy-start(f32[256,256]{1,0:T(8,128)} %param.12) | copy-start | bytes 786436
  272.1 5.4 %copy-start.4 = (f32[3,8,32,8,64]{4,3,1,2,0:T(8,128)S(1)}, f32[3,8,32,8,64]{4,3,1,2,0:T(8,128)}, u32[]{:S(2)}) copy-start(f32[3,8,32,8,64]{4,3,1,2,0:T(8,128)} %copy-done.3) | copy-start | bytes 4718596
  272.2 5.4 %copy-start.6 = (f32[8,256,64]{1,2,0:T(8,128)S(1)}, f32[8,256,64]{1,2,0:T(8,128)}, u32[]{:S(2)}) copy-start(f32[8,256,64]{1,2,0:T(8,128)} %copy.64) | copy-start | bytes 1572868
  272.2 5.4 %copy-start.7 = (f32[256,256]{1,0:T(8,128)S(1)}, f32[256,256]{1,0:T(8,128)}, u32[]{:S(2)}) copy-start(f32[256,256]{1,0:T(8,128)} %param.13) | copy-start | bytes 786436
  291.7 45.1 %all-to-all-start.2 = ((f32[32,1,12288]{2,1,0:T(1,128)}), f32[32,1,12288]{2,1,0:T(1,128)}, u32[]{:S(2)}, u32[]{:S(2)}) async-start(f32[32,1,12288]{2,1,0:T(1,128)} %reshape.21), calls=%async_computation.2 | async-start | bytes 3145728 | tf_op jit(solution)/shard_map/all_to_all | solution.py:34
  301.8 5.7 %copy-start.10 = (f32[256,256]{1,0:T(8,128)S(1)}, f32[256,256]{1,0:T(8,128)}, u32[]{:S(2)}) copy-start(f32[256,256]{1,0:T(8,128)} %param.10) | copy-start | bytes 786436
  351.7 3.3 copy-start.8
  368.9 27.2 %all-to-all-start.3 = ((f32[8,1,49152]{2,1,0:T(1,128)}), f32[8,1,49152]{2,1,0:T(1,128)}, u32[]{:S(2)}, u32[]{:S(2)}) async-start(f32[8,1,49152]{2,1,0:T(1,128)} %reshape.23), calls=%async_computation.3 | async-start | bytes 3145728 | tf_op jit(solution)/shard_map/all_to_all | solution.py:35
where the time goes:
time: 428 us; the launch traced here: 423 us
  local copies, waits for them, and re-layouts  145 us (34%)
  blocking collectives  140 us (33%)
  other arithmetic  50.4 us (12%)
  waiting for transfers between devices  38.5 us (9%)
  matrix products  37.1 us (9%)
  starting transfers between devices  11.1 us (3%)
    all_to_all x1, blocking collectives, on_device(): lax.all_to_all(onward, 'wide', split_axis=1, concat_axis=2, tiled=True)  82.5 us
    unnamed x30, local copies, waits for them, and re-layouts  60.2 us
    all_to_all x1, blocking collectives, on_device(): lax.all_to_all(bundle, 'narrow', split_axis=3, concat_axis=1, tiled=True)  57.8 us
    all_to_all x1, waiting for transfers between devices, on_device(): lax.all_to_all(part_z, 'wide', split_axis=2, concat_axis=1, tiled=True)  23.2 us
    dot_general x3, matrix products, contribution(): derived = jnp.einsum(formula, slopes, pair, precision=lax.Precision.HIGHEST)  19.2 us
    dot_general x3, matrix products, contribution(): jnp.einsum(formula, curves, fields, precision=lax.Precision.HIGHEST)  17.9 us
    all_to_all x1, waiting for transfers between devices, on_device(): lax.all_to_all(returned, 'narrow', split_axis=1, concat_axis=3, tiled=True)  15.3 us
    concatenate x1, local copies, waits for them, and re-layouts, on_device(): bundle = jnp.concatenate([velocity, extras], axis=0)  14.6 us
  transfers between devices with their start and end apart: 2, of which 2 were waited for; matrix products, arithmetic and copies ran while one was open for 5% of the time, Pallas kernels for 0%

commit v1 on v0

v1 whole, which is shorter than its diff:
```python
import functools

import jax
import jax.numpy as jnp
from jax import lax
from jax.experimental import pallas as pl
from jax.experimental.pallas import tpu as pltpu
from jax.sharding import PartitionSpec as P

MESH = pl.DeviceIdType.MESH
F32 = jnp.float32
BF16 = jnp.bfloat16
Z_ORDER = (2, 0, 1)
Y_ORDER = (1, 2, 0)
OUT_ORDER = (2, 0, 1)


def split(value):
    high = value.astype(BF16)
    return high, (value - high.astype(F32)).astype(BF16)


def product(left, right):
    dot = functools.partial(jnp.dot, preferred_element_type=F32)
    return dot(left[0], right[0]) + (dot(left[0], right[1]) + dot(left[1], right[0]))


def product_t(left, right):
    dot = functools.partial(lax.dot_general, dimension_numbers=(((1,), (1,)), ((), ())), preferred_element_type=F32)
    return dot(left[0], right[0]) + (dot(left[0], right[1]) + dot(left[1], right[0]))


def kernel(
    wide_size, narrow_size,
    vel, sx, cx, sy, cy, sz, cz,
    out,
    velv, opx, opyz, hx, lx, hyz, lyz,
    ysrc, zin, yin, zres, yres, zret, yret, acc,
    load_sem, send_sem, zin_sem, yin_sem, zret_sem, yret_sem, out_sem,
):
    wide = lax.axis_index("wide")
    narrow = lax.axis_index("narrow")
    rows, cols, width = velv.shape[1], velv.shape[2], velv.shape[3]

    load_vel = pltpu.make_async_copy(vel, velv, load_sem.at[0])
    load_vel.start()
    loads = [
        pltpu.make_async_copy(source, target, load_sem.at[1 + k])
        for k, (source, target) in enumerate(
            [(sx, opx.at[0]), (cx, opx.at[1]), (sy, opyz.at[0]), (cy, opyz.at[1]), (sz, opyz.at[2]), (cz, opyz.at[3])]
        )
    ]
    for load in loads:
        load.start()

    barrier = pltpu.get_barrier_semaphore()

    def greet_wide(k, carry):
        pl.semaphore_signal(barrier, inc=1, device_id={"wide": (wide + k) % wide_size}, device_id_type=MESH)
        return carry

    def greet_narrow(k, carry):
        pl.semaphore_signal(barrier, inc=1, device_id={"narrow": (narrow + k) % narrow_size}, device_id_type=MESH)
        return carry

    lax.fori_loop(1, wide_size, greet_wide, 0)
    lax.fori_loop(1, narrow_size, greet_narrow, 0)
    pl.semaphore_wait(barrier, wide_size + narrow_size - 2)

    z_rows = pl.ds(pl.multiple_of(wide * cols, cols), cols)
    y_rows = pl.ds(pl.multiple_of(narrow * rows, rows), rows)

    def send_z(c):
        def one(k, carry):
            to = (wide + k) % wide_size
            pltpu.make_async_remote_copy(
                vel.at[c, to], zin.at[c, z_rows], send_sem.at[0], zin_sem.at[c],
                device_id={"wide": to}, device_id_type=MESH,
            ).start()
            return carry

        lax.fori_loop(1, wide_size, one, 0)

    def send_y(c):
        def one(k, carry):
            to = (narrow + k) % narrow_size
            pltpu.make_async_remote_copy(
                ysrc.at[c, to], yin.at[c, y_rows], send_sem.at[1], yin_sem.at[c],
                device_id={"narrow": to}, device_id_type=MESH,
            ).start()
            return carry

        lax.fori_loop(1, narrow_size, one, 0)

    def return_z(c):
        def one(k, carry):
            to = (wide + k) % wide_size
            pltpu.make_async_remote_copy(
                zres.at[c, pl.ds(pl.multiple_of(to * cols, cols), cols)], zret.at[c, wide], send_sem.at[2], zret_sem.at[c],
                device_id={"wide": to}, device_id_type=MESH,
            ).start()
            return carry

        lax.fori_loop(1, wide_size, one, 0)

    def return_y(c):
        def one(k, carry):
            to = (narrow + k) % narrow_size
            pltpu.make_async_remote_copy(
                yres.at[c, pl.ds(pl.multiple_of(to * rows, rows), rows)], yret.at[c, narrow], send_sem.at[3], yret_sem.at[c],
                device_id={"narrow": to}, device_id_type=MESH,
            ).start()
            return carry

        lax.fori_loop(1, narrow_size, one, 0)

    def lines_up(c):
        for n in range(narrow_size):
            ysrc[c, n] = velv[c, :, n, :]
        yin[c, y_rows] = ysrc[c, narrow]
        zin[c, z_rows] = velv[c, wide]

    send_z(Z_ORDER[0])
    load_vel.wait()
    lines_up(Y_ORDER[0])
    send_y(Y_ORDER[0])
    send_z(Z_ORDER[1])
    lines_up(Y_ORDER[1])
    send_y(Y_ORDER[1])
    send_z(Z_ORDER[2])
    lines_up(Y_ORDER[2])
    send_y(Y_ORDER[2])

    for load in loads:
        load.wait()
    for k in range(2):
        hx[k], lx[k] = split((-0.5, 0.5)[k] * opx[k])
    for k in range(4):
        hyz[k], lyz[k] = split((-0.5, 0.5)[k % 2] * opyz[k])

    def x_part(c, carry):
        along = velv[0].reshape(rows * cols, width)
        field = velv[c].reshape(rows * cols, width)
        pair = split(field)
        total = product_t(split(field * along), (hx[0], lx[0])) + product_t(pair, (hx[1], lx[1]))
        total = total + along * product_t(pair, (hx[0], lx[0]))
        acc[c] = total.reshape(rows, cols, width)
        return carry

    lax.fori_loop(0, 3, x_part, 0)

    def line_part(source, result, operators, direction, c):
        slope, curve = (hyz[operators], lyz[operators]), (hyz[operators + 1], lyz[operators + 1])
        along, field = source[direction], source[c]
        pair = split(field)
        total = product(slope, split(field * along)) + product(curve, pair)
        result[c] = total + along * product(slope, pair)

    def arrived(sem, buffer, blocks, size):
        part = buffer.at[pl.ds(0, (blocks - 1) * size)]
        pltpu.make_async_copy(part, part, sem).wait()

    for step in range(3):
        c = Z_ORDER[step]
        arrived(zin_sem.at[c], zin.at[c], wide_size, cols)
        line_part(zin, zres, 2, 2, c)
        return_z(c)
        zret[c, wide] = zres[c, z_rows]
        c = Y_ORDER[step]
        arrived(yin_sem.at[c], yin.at[c], narrow_size, rows)
        line_part(yin, yres, 0, 1, c)
        return_y(c)
        yret[c, narrow] = yres[c, y_rows]

    writes = []
    for c in OUT_ORDER:
        arrived(zret_sem.at[c], zret.at[c], wide_size, 1)
        acc[c] = acc[c] + zret[c]
        arrived(yret_sem.at[c], yret.at[c], narrow_size, 1)
        for n in range(narrow_size):
            acc[c, :, n, :] = acc[c, :, n, :] + yret[c, n]
        write = pltpu.make_async_copy(acc.at[c], out.at[c], out_sem.at[c])
        write.start()
        writes.append(write)

    for sem, buffer, blocks, size in (
        (send_sem.at[0], zin, wide_size, cols),
        (send_sem.at[1], yin, narrow_size, rows),
        (send_sem.at[2], zin, wide_size, cols),
        (send_sem.at[3], yin, narrow_size, rows),
    ):
        part = buffer.at[:, pl.ds(0, (blocks - 1) * size)]
        pltpu.make_async_copy(part, part, sem).wait()
    for write in writes:
        write.wait()


def on_device(wide_size, narrow_size, velocity, slope_x, curve_x, slope_y, curve_y, slope_z, curve_z):
    _, rows, cols, width = velocity.shape
    z_lines, y_lines = wide_size * cols, narrow_size * rows
    dma = pltpu.SemaphoreType.DMA
    return pl.pallas_call(
        functools.partial(kernel, wide_size, narrow_size),
        out_shape=jax.ShapeDtypeStruct(velocity.shape, F32),
        in_specs=[pl.BlockSpec(memory_space=pl.ANY)] * 7,
        out_specs=pl.BlockSpec(memory_space=pl.ANY),
        scratch_shapes=[
            pltpu.VMEM(velocity.shape, F32),
            pltpu.VMEM((2, width, width), F32),
            pltpu.VMEM((4, z_lines, z_lines), F32),
            pltpu.VMEM((2, width, width), BF16),
            pltpu.VMEM((2, width, width), BF16),
            pltpu.VMEM((4, z_lines, z_lines), BF16),
            pltpu.VMEM((4, z_lines, z_lines), BF16),
            pltpu.VMEM((3, cols, rows, width), F32),
            pltpu.VMEM((3, z_lines, width), F32),
            pltpu.VMEM((3, y_lines, width), F32),
            pltpu.VMEM((3, z_lines, width), F32),
            pltpu.VMEM((3, y_lines, width), F32),
            pltpu.VMEM(velocity.shape, F32),
            pltpu.VMEM((3, cols, rows, width), F32),
            pltpu.VMEM(velocity.shape, F32),
            dma((7,)),
            dma((4,)),
            dma((3,)),
            dma((3,)),
            dma((3,)),
            dma((3,)),
            dma((3,)),
        ],
        compiler_params=pltpu.CompilerParams(
            collective_id=0, has_side_effects=True, vmem_limit_bytes=48 * 1024 * 1024
        ),
    )(velocity, slope_x, curve_x, slope_y, curve_y, slope_z, curve_z)


def solution(mesh):
    return jax.shard_map(
        functools.partial(on_device, mesh.shape["wide"], mesh.shape["narrow"]),
        mesh=mesh,
        in_specs=(P(None, "narrow", "wide", None), P(), P(), P(), P(), P(), P()),
        out_specs=P(None, "narrow", "wide", None),
        check_vma=False,
    )
```

time: 428 us -> 90.7 us (0.21); the launches traced: 423 us -> 90.5 us
  blocking collectives: 140 us -> 0 us
  local copies, waits for them, and re-layouts: 145 us -> 7.39 us
  Pallas kernels: 0 us -> 83.1 us
  other arithmetic: 50.4 us -> 0 us
  waiting for transfers between devices: 38.5 us -> 0 us
  matrix products: 37.1 us -> 0 us
  starting transfers between devices: 11.1 us -> 0 us
    all_to_all x2 -> x0, blocking collectives: 140 us -> none  [the longest x1 82.5 us: on_device(): lax.all_to_all(onward, 'wide', split_axis=1, concat_axis=2, tiled=True)]
    pallas_call x0 -> x1, Pallas kernels: none -> 83.1 us  [on_device(): pl.pallas_call(functools.partial(kernel, wide_size, narrow_size), out_sha...]
    unnamed x30 -> x13, local copies, waits for them, and re-layouts: 60.2 us -> 7.39 us
    all_to_all x4 -> x0, other arithmetic: 39.7 us -> none  [the longest x1 13.7 us: on_device(): lax.all_to_all(bundle, 'narrow', split_axis=3, concat_axis=1, tiled=True)]
    all_to_all x2 -> x0, waiting for transfers between devices: 38.5 us -> none  [the longest x1 23.2 us: on_device(): lax.all_to_all(part_z, 'wide', split_axis=2, concat_axis=1, tiled=True)]
    dot_general x6 -> x0, matrix products: 37.1 us -> none  [the longest x3 19.2 us: contribution(): derived = jnp.einsum(formula, slopes, pair, precision=lax.Precision.HIGHEST)]
    all_to_all x7 -> x0, local copies, waits for them, and re-layouts: 33.3 us -> none  [the longest x2 13.3 us: on_device(): lax.all_to_all(bundle, 'narrow', split_axis=3, concat_axis=1, tiled=True)]
    slice x8 -> x0, local copies, waits for them, and re-layouts: 23.4 us -> none  [the longest x2 6.68 us: on_device(): gathered_z[:3]]
  transfers between devices with their start and end apart: 2 -> 0, of which waited for: 2 -> 0; matrix products, arithmetic and copies ran while one was open for 5% -> 0% of each run, Pallas kernels for 0% -> 0%
where the time goes in v1:
time: 90.7 us; the launch traced here: 90.5 us
  Pallas kernels  83.1 us (92%)
  local copies, waits for them, and re-layouts  7.39 us (8%)
    pallas_call x1, Pallas kernels, on_device(): pl.pallas_call(functools.partial(kernel, wide_size, narrow_size), out_sha...  83.1 us
    unnamed x13, local copies, waits for them, and re-layouts  7.39 us

profile of v1, /device:TPU:1, one launch (start us, length us, event | category | flops | bytes accessed | tf_op | source)
XLA Modules:
  0.0 90.5 jit_solution(12526547633457851026)
XLA Ops:
  0.0 0.0 copy-start
  0.0 1.2 %copy-done = f32[512,512]{1,0:T(8,128)S(1)} copy-done((f32[512,512]{1,0:T(8,128)S(1)}, f32[512,512]{1,0:T(8,128)}, u32[]{:S(2)}) %copy-start) | copy-done | bytes 1048600
  1.2 0.0 copy-start.1
  1.2 1.2 %copy-done.1 = f32[512,512]{1,0:T(8,128)S(1)} copy-done((f32[512,512]{1,0:T(8,128)S(1)}, f32[512,512]{1,0:T(8,128)}, u32[]{:S(2)}) %copy-start.1) | copy-done | bytes 1048600
  2.5 0.0 copy-start.2
  2.5 0.9 %copy-done.2 = f32[256,256]{1,0:T(8,128)S(1)} copy-done((f32[256,256]{1,0:T(8,128)S(1)}, f32[256,256]{1,0:T(8,128)}, u32[]{:S(2)}) %copy-start.2) | copy-done | bytes 262168
  3.4 0.0 copy-start.3
  3.4 0.9 %copy-done.3 = f32[256,256]{1,0:T(8,128)S(1)} copy-done((f32[256,256]{1,0:T(8,128)S(1)}, f32[256,256]{1,0:T(8,128)}, u32[]{:S(2)}) %copy-start.3) | copy-done | bytes 262168
  4.4 0.0 copy-start.4
  4.4 0.9 %copy-done.4 = f32[256,256]{1,0:T(8,128)S(1)} copy-done((f32[256,256]{1,0:T(8,128)S(1)}, f32[256,256]{1,0:T(8,128)}, u32[]{:S(2)}) %copy-start.4) | copy-done | bytes 262168
  5.3 0.0 copy-start.5
  5.3 0.9 %copy-done.5 = f32[256,256]{1,0:T(8,128)S(1)} copy-done((f32[256,256]{1,0:T(8,128)S(1)}, f32[256,256]{1,0:T(8,128)}, u32[]{:S(2)}) %copy-start.5) | copy-done | bytes 262168
  6.3 83.1 %shard_map.73 = f32[3,32,8,512]{3,2,1,0:T(8,128)S(1)} custom-call(f32[3,32,8,512]{3,2,1,0:T(8,128)} %vel.1, f32[512,512]{1,0:T(8,128)S(1)} %copy-done, f32[512,512]{1,0:T(8,128)S(1)} %copy-done.1, f32[256,256]{1,0:T(8,128)S(1)} %copy-done.2, f32[256,256]{1,0:T(8,128)S(1)} %copy-done.3, f32[256,256]{1,0:T(8,128)S(1)} %copy-done.4, f32[256,256]{1,0:T(8,128)S(1)} %copy-done.5), custom_call_target="tpu_custom_call" | custom-call | tf_op jit(solution)/shard_map/pallas_call | solution.py:202
  89.3 1.1 %copy.9 = f32[3,32,8,512]{3,2,1,0:T(8,128)} copy(f32[3,32,8,512]{3,2,1,0:T(8,128)S(1)} %shard_map.73) | data formatting | bytes 3145728
Async XLA Ops:
  0.0 1.2 %copy-start = (f32[512,512]{1,0:T(8,128)S(1)}, f32[512,512]{1,0:T(8,128)}, u32[]{:S(2)}) copy-start(f32[512,512]{1,0:T(8,128)} %sx.1) | copy-start | bytes 3145732
  1.2 1.2 %copy-start.1 = (f32[512,512]{1,0:T(8,128)S(1)}, f32[512,512]{1,0:T(8,128)}, u32[]{:S(2)}) copy-start(f32[512,512]{1,0:T(8,128)} %cx.1) | copy-start | bytes 3145732
  2.5 0.9 %copy-start.2 = (f32[256,256]{1,0:T(8,128)S(1)}, f32[256,256]{1,0:T(8,128)}, u32[]{:S(2)}) copy-start(f32[256,256]{1,0:T(8,128)} %sy.1) | copy-start | bytes 786436
  3.4 0.9 %copy-start.3 = (f32[256,256]{1,0:T(8,128)S(1)}, f32[256,256]{1,0:T(8,128)}, u32[]{:S(2)}) copy-start(f32[256,256]{1,0:T(8,128)} %cy.1) | copy-start | bytes 786436
  4.4 0.9 %copy-start.4 = (f32[256,256]{1,0:T(8,128)S(1)}, f32[256,256]{1,0:T(8,128)}, u32[]{:S(2)}) copy-start(f32[256,256]{1,0:T(8,128)} %sz.1) | copy-start | bytes 786436
  5.3 0.9 %copy-start.5 = (f32[256,256]{1,0:T(8,128)S(1)}, f32[256,256]{1,0:T(8,128)}, u32[]{:S(2)}) copy-start(f32[256,256]{1,0:T(8,128)} %cz.1) | copy-start | bytes 786436

commit v2 on v1

--- a/solution.py
+++ b/solution.py
@@ -12,7 +12,6 @@
 BF16 = jnp.bfloat16
 Z_ORDER = (2, 0, 1)
 Y_ORDER = (1, 2, 0)
-OUT_ORDER = (2, 0, 1)
 
 
 def split(value):
@@ -33,10 +32,10 @@
 def kernel(
     wide_size, narrow_size,
     vel, sx, cx, sy, cy, sz, cz,
-    out,
+    acc,
     velv, opx, opyz, hx, lx, hyz, lyz,
-    ysrc, zin, yin, zres, yres, zret, yret, acc,
-    load_sem, send_sem, zin_sem, yin_sem, zret_sem, yret_sem, out_sem,
+    ysrc, zin, yin, zres, yres, yret, zret,
+    load_sem, send_sem, zin_sem, yin_sem, zret_sem, yret_sem,
 ):
     wide = lax.axis_index("wide")
     narrow = lax.axis_index("narrow")
@@ -54,16 +53,24 @@
         load.start()
 
     barrier = pltpu.get_barrier_semaphore()
+    deep = wide_size // 4
+    y_lo, z, core = wide // (2 * deep), (wide // 2) % deep, wide % 2
+
+    def wide_peer(k):
+        turn = k // 4
+        far = (deep // 2 - (turn + 1) // 2) * (1 - 2 * ((turn + 1 + core) % 2))
+        other_y, other_core = 1 - (k % 4) // 2, 1 - k % 2
+        return ((y_lo + other_y) % 2 * deep + (z + far + deep) % deep) * 2 + (core + other_core) % 2
 
     def greet_wide(k, carry):
-        pl.semaphore_signal(barrier, inc=1, device_id={"wide": (wide + k) % wide_size}, device_id_type=MESH)
+        pl.semaphore_signal(barrier, inc=1, device_id={"wide": wide_peer(k)}, device_id_type=MESH)
         return carry
 
     def greet_narrow(k, carry):
         pl.semaphore_signal(barrier, inc=1, device_id={"narrow": (narrow + k) % narrow_size}, device_id_type=MESH)
         return carry
 
-    lax.fori_loop(1, wide_size, greet_wide, 0)
+    lax.fori_loop(0, wide_size - 1, greet_wide, 0)
     lax.fori_loop(1, narrow_size, greet_narrow, 0)
     pl.semaphore_wait(barrier, wide_size + narrow_size - 2)
 
@@ -72,14 +79,14 @@
 
     def send_z(c):
         def one(k, carry):
-            to = (wide + k) % wide_size
+            to = wide_peer(k)
             pltpu.make_async_remote_copy(
                 vel.at[c, to], zin.at[c, z_rows], send_sem.at[0], zin_sem.at[c],
                 device_id={"wide": to}, device_id_type=MESH,
             ).start()
             return carry
 
-        lax.fori_loop(1, wide_size, one, 0)
+        lax.fori_loop(0, wide_size - 1, one, 0)
 
     def send_y(c):
         def one(k, carry):
@@ -94,14 +101,14 @@
 
     def return_z(c):
         def one(k, carry):
-            to = (wide + k) % wide_size
+            to = wide_peer(k)
             pltpu.make_async_remote_copy(
                 zres.at[c, pl.ds(pl.multiple_of(to * cols, cols), cols)], zret.at[c, wide], send_sem.at[2], zret_sem.at[c],
                 device_id={"wide": to}, device_id_type=MESH,
             ).start()
             return carry
 
-        lax.fori_loop(1, wide_size, one, 0)
+        lax.fori_loop(0, wide_size - 1, one, 0)
 
     def return_y(c):
         def one(k, carry):
@@ -172,16 +179,13 @@
         return_y(c)
         yret[c, narrow] = yres[c, y_rows]
 
-    writes = []
-    for c in OUT_ORDER:
-        arrived(zret_sem.at[c], zret.at[c], wide_size, 1)
-        acc[c] = acc[c] + zret[c]
+    for c in Y_ORDER:
         arrived(yret_sem.at[c], yret.at[c], narrow_size, 1)
         for n in range(narrow_size):
             acc[c, :, n, :] = acc[c, :, n, :] + yret[c, n]
-        write = pltpu.make_async_copy(acc.at[c], out.at[c], out_sem.at[c])
-        write.start()
-        writes.append(write)
+    for c in Z_ORDER:
+        arrived(zret_sem.at[c], zret.at[c], wide_size, 1)
+        acc[c] = acc[c] + zret[c]
 
     for sem, buffer, blocks, size in (
         (send_sem.at[0], zin, wide_size, cols),
@@ -191,8 +195,6 @@
     ):
         part = buffer.at[:, pl.ds(0, (blocks - 1) * size)]
         pltpu.make_async_copy(part, part, sem).wait()
-    for write in writes:
-        write.wait()
 
 
 def on_device(wide_size, narrow_size, velocity, slope_x, curve_x, slope_y, curve_y, slope_z, curve_z):
@@ -202,8 +204,8 @@
     return pl.pallas_call(
         functools.partial(kernel, wide_size, narrow_size),
         out_shape=jax.ShapeDtypeStruct(velocity.shape, F32),
-        in_specs=[pl.BlockSpec(memory_space=pl.ANY)] * 7,
-        out_specs=pl.BlockSpec(memory_space=pl.ANY),
+        in_specs=[pl.BlockSpec(memory_space=pltpu.HBM)] * 7,
+        out_specs=pl.BlockSpec(memory_space=pltpu.VMEM),
         scratch_shapes=[
             pltpu.VMEM(velocity.shape, F32),
             pltpu.VMEM((2, width, width), F32),
@@ -217,7 +219,6 @@
             pltpu.VMEM((3, y_lines, width), F32),
             pltpu.VMEM((3, z_lines, width), F32),
             pltpu.VMEM((3, y_lines, width), F32),
-            pltpu.VMEM(velocity.shape, F32),
             pltpu.VMEM((3, cols, rows, width), F32),
             pltpu.VMEM(velocity.shape, F32),
             dma((7,)),
@@ -226,12 +227,11 @@
             dma((3,)),
             dma((3,)),
             dma((3,)),
-            dma((3,)),
         ],
         compiler_params=pltpu.CompilerParams(
-            collective_id=0, has_side_effects=True, vmem_limit_bytes=48 * 1024 * 1024
+            collective_id=0, has_side_effects=True, vmem_limit_bytes=40 * 1024 * 1024
         ),
-    )(velocity, slope_x, curve_x, slope_y, curve_y, slope_z, curve_z)
+    )(*[pltpu.with_memory_space_constraint(a, pltpu.HBM) for a in (velocity, slope_x, curve_x, slope_y, curve_y, slope_z, curve_z)])
 
 
 def solution(mesh):

time: 90.7 us -> 84.5 us (0.932)
  local copies, waits for them, and re-layouts: 7.39 us -> 1.15 us
    unnamed x13 -> x1, local copies, waits for them, and re-layouts: 7.39 us -> 1.15 us
where the time goes in v2:
time: 84.5 us
  Pallas kernels  83.3 us (99%)
  local copies, waits for them, and re-layouts  1.15 us (1%)
    pallas_call x1, Pallas kernels, on_device(): pl.pallas_call(functools.partial(kernel, wide_size, narrow_size), out_sha...  83.3 us

profile of v2, /device:TPU:1, one launch (start us, length us, event | category | flops | bytes accessed | tf_op | source)
XLA Modules:
  0.0 84.5 jit_solution(3146740485687579247)
XLA Ops:
  0.0 83.3 %shard_map.73 = f32[3,32,8,512]{3,2,1,0:T(8,128)S(1)} custom-call(f32[3,32,8,512]{3,2,1,0:T(8,128)} %vel.1, f32[512,512]{1,0:T(8,128)} %sx.1, f32[512,512]{1,0:T(8,128)} %cx.1, f32[256,256]{1,0:T(8,128)} %sy.1, f32[256,256]{1,0:T(8,128)} %cy.1, f32[256,256]{1,0:T(8,128)} %sz.1, f32[256,256]{1,0:T(8,128)} %cz.1), custom_call_target="tpu_custom_call" | custom-call | tf_op jit(solution)/shard_map/pallas_call | solution.py:204
  83.3 1.1 %copy.9 = f32[3,32,8,512]{3,2,1,0:T(8,128)} copy(f32[3,32,8,512]{3,2,1,0:T(8,128)S(1)} %shard_map.73) | data formatting | bytes 3145728

commit v3 on v0

v3 whole, which is shorter than its diff:
```python
import functools

import jax
import jax.numpy as jnp
from jax import lax
from jax.experimental import pallas as pl
from jax.experimental.pallas import tpu as pltpu
from jax.sharding import PartitionSpec as P

MESH = pl.DeviceIdType.MESH
F32 = jnp.float32
BF16 = jnp.bfloat16


def split(value):
    high = value.astype(BF16)
    return high, (value - high.astype(F32)).astype(BF16)


def product(left, right):
    dot = functools.partial(jnp.dot, preferred_element_type=F32)
    return dot(left[0], right[0]) + (dot(left[0], right[1]) + dot(left[1], right[0]))


def product_t(left, right):
    dot = functools.partial(lax.dot_general, dimension_numbers=(((1,), (1,)), ((), ())), preferred_element_type=F32)
    return dot(left[0], right[0]) + (dot(left[0], right[1]) + dot(left[1], right[0]))


def kernel(
    wide_size, narrow_size,
    vel, sx, cx, sy, cy, sz, cz,
    acc,
    velv, opx, opyz, hx, lx, hyz, lyz,
    pin, qin, ysp, ysq, zin, yin, zres, yres,
    zret_p, zret_o, yret_p, yret_q, psum, back_p, back_q,
    load_sem, send_sem, pin_sem, qin_sem, zin_sem, yin_sem,
    zret_p_sem, zret_o_sem, yret_p_sem, yret_q_sem, back_p_sem, back_q_sem,
):
    wide = lax.axis_index("wide")
    narrow = lax.axis_index("narrow")
    rows, cols, width = velv.shape[1], velv.shape[2], velv.shape[3]
    half = width // 2
    deep, across = wide_size // 4, narrow_size // 2
    group = 2 * deep
    y_lo, place, core = wide // group, wide % group, wide % 2
    z = place // 2
    y_hi, x = narrow // across, narrow % across
    p_wide = (1 - y_lo) * group + place
    q_narrow = (1 - y_hi) * across + x
    p_device = {"wide": p_wide}
    q_device = {"wide": p_wide, "narrow": q_narrow}
    kept = (y_hi + y_lo) % 2
    keep = pl.ds(pl.multiple_of(kept * half, 128), half)
    give = pl.ds(pl.multiple_of((1 - kept) * half, 128), half)
    line_rows, planes = rows // group, cols // across

    def z_peer(k):
        turn = k // 2
        far = (deep // 2 - (turn + 1) // 2) * (1 - 2 * ((turn + 1 + core) % 2))
        return (z + far + deep) % deep * 2 + (core + 1 - k % 2) % 2

    def to_place(place_to):
        return {"wide": y_lo * group + place_to}

    def to_x(x_to):
        return {"narrow": y_hi * across + x_to}

    barrier = pltpu.get_barrier_semaphore()

    def greet(k, carry):
        pl.semaphore_signal(barrier, inc=1, device_id=to_place(z_peer(k)), device_id_type=MESH)
        return carry

    lax.fori_loop(0, group - 1, greet, 0)
    for k in range(1, across):
        pl.semaphore_signal(barrier, inc=1, device_id=to_x((x + k) % across), device_id_type=MESH)
    pl.semaphore_signal(barrier, inc=1, device_id=p_device, device_id_type=MESH)
    pl.semaphore_signal(barrier, inc=1, device_id=q_device, device_id_type=MESH)

    load_vel = pltpu.make_async_copy(vel, velv, load_sem.at[0])
    load_vel.start()
    loads = [
        pltpu.make_async_copy(source, target, load_sem.at[1 + k])
        for k, (source, target) in enumerate(
            [(sx, opx.at[0]), (cx, opx.at[1]), (sy, opyz.at[0]), (cy, opyz.at[1]), (sz, opyz.at[2]), (cz, opyz.at[3])]
        )
    ]
    for load in loads:
        load.start()
    pl.semaphore_wait(barrier, group + across)

    def block(index, size):
        return pl.ds(pl.multiple_of(index * size, size), size)

    def send(source, target, sent, landed, device):
        pltpu.make_async_remote_copy(
            source, target, send_sem.at[sent], landed, device_id=device, device_id_type=MESH
        ).start()

    def each_place(one):
        def step(k, carry):
            one(z_peer(k))
            return carry

        lax.fori_loop(0, group - 1, step, 0)

    def send_p(c):
        send(vel.at[c, :, :, give], pin.at[c], 0, pin_sem.at[c], p_device)

    def send_q(c):
        send(vel.at[c, :, :, keep], qin.at[c], 1, qin_sem.at[c], q_device)

    def send_z_own(c):
        def one(to):
            send(vel.at[c, block(to, line_rows), :, keep], zin.at[c, :, block(wide, cols)], 2, zin_sem.at[c], to_place(to))

        each_place(one)

    def send_z_p(c):
        def one(to):
            send(pin.at[c, block(to, line_rows)], zin.at[c, :, block(p_wide, cols)], 2, zin_sem.at[c], to_place(to))

        each_place(one)
        zin[c, :, block(p_wide, cols)] = pin[c, block(place, line_rows)]

    def send_y(c, source, turned, from_narrow):
        for plane in range(cols):
            turned[c, plane] = source[c, :, plane, :]
        for k in range(1, across):
            to = (x + k) % across
            send(turned.at[c, block(to, planes)], yin.at[c, :, block(from_narrow, rows)], 3, yin_sem.at[c], to_x(to))
        yin[c, :, block(from_narrow, rows)] = turned[c, block(x, planes)]

    def arrived(part, sem):
        pltpu.make_async_copy(part, part, sem).wait()

    def line_part(source, result, operators, direction, c, count):
        slope, curve = (hyz[operators], lyz[operators]), (hyz[operators + 1], lyz[operators + 1])

        def one(k, carry):
            along, field = source[direction, k], source[c, k]
            pair = split(field)
            total = product(slope, split(field * along)) + product(curve, pair)
            result[c, k] = total + along * product(slope, pair)
            return carry

        lax.fori_loop(0, count, one, 0)

    def x_part(c):
        along = velv[0].reshape(rows * cols, width)
        field = velv[c].reshape(rows * cols, width)
        pair = split(field)
        total = product_t(split(field * along), (hx[0], lx[0])) + product_t(pair, (hx[1], lx[1]))
        total = total + along * product_t(pair, (hx[0], lx[0]))
        acc[c] = total.reshape(rows, cols, width)

    def z_part(c):
        arrived(zin.at[c, :, pl.ds(0, 2 * (group - 1) * cols)], zin_sem.at[c])
        line_part(zin, zres, 2, 2, c, line_rows)

        def one_p(to):
            send(zres.at[c, :, block((1 - y_lo) * group + to, cols)], zret_p.at[c, block(place, line_rows)], 4, zret_p_sem.at[c], to_place(to))

        def one_o(to):
            send(zres.at[c, :, block(y_lo * group + to, cols)], zret_o.at[c, block(place, line_rows)], 4, zret_o_sem.at[c], to_place(to))

        each_place(one_p)
        each_place(one_o)
        zret_p[c, block(place, line_rows)] = zres[c, :, block(p_wide, cols)]
        zret_o[c, block(place, line_rows)] = zres[c, :, block(wide, cols)]

    def y_part(c):
        if across > 1:
            arrived(yin.at[c, :, pl.ds(0, 2 * (across - 1) * rows)], yin_sem.at[c])
        line_part(yin, yres, 0, 1, c, planes)
        for k in range(1, across):
            to = (x + k) % across
            send(yres.at[c, :, block((1 - y_hi) * across + to, rows)], yret_q.at[c, block(x, planes)], 5, yret_q_sem.at[c], to_x(to))
        for k in range(1, across):
            to = (x + k) % across
            send(yres.at[c, :, block(y_hi * across + to, rows)], yret_p.at[c, block(x, planes)], 5, yret_p_sem.at[c], to_x(to))
        yret_q[c, block(x, planes)] = yres[c, :, block(q_narrow, rows)]
        yret_p[c, block(x, planes)] = yres[c, :, block(narrow, rows)]

    def back_to_q(c):
        if across > 1:
            arrived(yret_q.at[c, pl.ds(0, (across - 1) * planes)], yret_q_sem.at[c])
        send(yret_q.at[c], back_q.at[c], 6, back_q_sem.at[c], q_device)

    def back_to_p(c):
        if across > 1:
            arrived(yret_p.at[c, pl.ds(0, (across - 1) * planes)], yret_p_sem.at[c])
        arrived(zret_p.at[c, pl.ds(0, (group - 1) * line_rows)], zret_p_sem.at[c])
        for plane in range(cols):
            psum[c, :, plane, :] = zret_p[c, :, plane, :] + yret_p[c, plane]
        send(psum.at[c], back_p.at[c], 7, back_p_sem.at[c], p_device)

    def add_q(c):
        arrived(back_q.at[c], back_q_sem.at[c])
        for plane in range(cols):
            acc[c, :, plane, keep] = acc[c, :, plane, keep] + back_q[c, plane]

    def add_p(c):
        arrived(back_p.at[c], back_p_sem.at[c])
        acc[c, :, :, give] = acc[c, :, :, give] + back_p[c]

    def add_own(c):
        arrived(zret_o.at[c, pl.ds(0, (group - 1) * line_rows)], zret_o_sem.at[c])
        acc[c, :, :, keep] = acc[c, :, :, keep] + zret_o[c]

    send_p(2)
    send_z_own(2)
    send_q(1)
    send_p(1)
    send_z_own(1)
    send_q(2)
    send_p(0)
    send_z_own(0)
    send_q(0)

    load_vel.wait()
    for c in range(3):
        zin[c, :, block(wide, cols)] = velv[c, block(place, line_rows), :, keep]
    for load in loads:
        load.wait()
    for k in range(2):
        hx[k], lx[k] = split((-0.5, 0.5)[k] * opx[k])
    for k in range(4):
        hyz[k], lyz[k] = split((-0.5, 0.5)[k % 2] * opyz[k])

    arrived(pin.at[2], pin_sem.at[2])
    send_z_p(2)
    x_part(2)
    arrived(pin.at[1], pin_sem.at[1])
    send_y(1, pin, ysp, narrow)
    send_z_p(1)
    arrived(qin.at[1], qin_sem.at[1])
    send_y(1, qin, ysq, q_narrow)
    send_y(2, pin, ysp, narrow)
    x_part(1)
    arrived(pin.at[0], pin_sem.at[0])
    send_z_p(0)
    send_y(0, pin, ysp, narrow)
    arrived(qin.at[2], qin_sem.at[2])
    send_y(2, qin, ysq, q_narrow)
    arrived(qin.at[0], qin_sem.at[0])
    send_y(0, qin, ysq, q_narrow)
    x_part(0)

    z_part(2)
    y_part(1)
    y_part(2)
    back_to_q(1)
    z_part(1)
    y_part(0)
    back_to_q(2)
    z_part(0)
    back_to_q(0)
    back_to_p(2)
    add_q(1)
    add_q(2)
    back_to_p(1)
    add_q(0)
    add_p(2)
    add_own(2)
    back_to_p(0)
    add_p(1)
    add_own(1)
    add_p(0)
    add_own(0)

    parts = [pin, qin, zin.at[:, :, pl.ds(0, 2 * (group - 1) * cols)]] * 2
    for k, part in ((0, pin), (1, qin), (2, parts[2]), (4, parts[2]), (6, back_q), (7, back_p)):
        arrived(part, send_sem.at[k])
    if across > 1:
        for k in (3, 5):
            arrived(yin.at[:, :, pl.ds(0, 2 * (across - 1) * rows)], send_sem.at[k])


def on_device(wide_size, narrow_size, *arrays):
    shape = arrays[0].shape
    _, rows, cols, width = shape
    group, across, half = wide_size // 2, narrow_size // 2, width // 2
    z_lines, y_lines = wide_size * cols, narrow_size * rows
    vmem, dma = pltpu.VMEM, pltpu.SemaphoreType.DMA
    part, turned = vmem((3, rows, cols, half), F32), vmem((3, cols, rows, half), F32)
    z_block, y_block = vmem((3, rows // group, z_lines, half), F32), vmem((3, cols // across, y_lines, half), F32)
    return pl.pallas_call(
        functools.partial(kernel, wide_size, narrow_size),
        out_shape=jax.ShapeDtypeStruct(shape, F32),
        in_specs=[pl.BlockSpec(memory_space=pltpu.HBM)] * 7,
        out_specs=pl.BlockSpec(memory_space=pltpu.VMEM),
        scratch_shapes=[
            vmem(shape, F32),
            vmem((2, width, width), F32),
            vmem((4, z_lines, z_lines), F32),
            vmem((2, width, width), BF16),
            vmem((2, width, width), BF16),
            vmem((4, z_lines, z_lines), BF16),
            vmem((4, z_lines, z_lines), BF16),
            part, part, turned, turned, z_block, y_block, z_block, y_block,
            part, part, turned, turned, part, part, turned,
            dma((7,)),
            dma((8,)),
            *[dma((3,))] * 10,
        ],
        compiler_params=pltpu.CompilerParams(
            collective_id=0, has_side_effects=True, vmem_limit_bytes=40 * 1024 * 1024
        ),
    )(*[pltpu.with_memory_space_constraint(array, pltpu.HBM) for array in arrays])


def solution(mesh):
    return jax.shard_map(
        functools.partial(on_device, mesh.shape["wide"], mesh.shape["narrow"]),
        mesh=mesh,
        in_specs=(P(None, "narrow", "wide", None), P(), P(), P(), P(), P(), P()),
        out_specs=P(None, "narrow", "wide", None),
        check_vma=False,
    )
```

time: 428 us -> 82.4 us (0.19); the launches traced: 423 us -> 82.3 us
  local copies, waits for them, and re-layouts: 145 us -> 1.15 us
  blocking collectives: 140 us -> 0 us
  Pallas kernels: 0 us -> 81.2 us
  other arithmetic: 50.4 us -> 0 us
  waiting for transfers between devices: 38.5 us -> 0 us
  matrix products: 37.1 us -> 0 us
  starting transfers between devices: 11.1 us -> 0 us
    all_to_all x2 -> x0, blocking collectives: 140 us -> none  [the longest x1 82.5 us: on_device(): lax.all_to_all(onward, 'wide', split_axis=1, concat_axis=2, tiled=True)]
    pallas_call x0 -> x1, Pallas kernels: none -> 81.2 us  [on_device(): pl.pallas_call(functools.partial(kernel, wide_size, narrow_size), out_sha...]
    unnamed x30 -> x1, local copies, waits for them, and re-layouts: 60.2 us -> 1.15 us
    all_to_all x4 -> x0, other arithmetic: 39.7 us -> none  [the longest x1 13.7 us: on_device(): lax.all_to_all(bundle, 'narrow', split_axis=3, concat_axis=1, tiled=True)]
    all_to_all x2 -> x0, waiting for transfers between devices: 38.5 us -> none  [the longest x1 23.2 us: on_device(): lax.all_to_all(part_z, 'wide', split_axis=2, concat_axis=1, tiled=True)]
    dot_general x6 -> x0, matrix products: 37.1 us -> none  [the longest x3 19.2 us: contribution(): derived = jnp.einsum(formula, slopes, pair, precision=lax.Precision.HIGHEST)]
    all_to_all x7 -> x0, local copies, waits for them, and re-layouts: 33.3 us -> none  [the longest x2 13.3 us: on_device(): lax.all_to_all(bundle, 'narrow', split_axis=3, concat_axis=1, tiled=True)]
    slice x8 -> x0, local copies, waits for them, and re-layouts: 23.4 us -> none  [the longest x2 6.68 us: on_device(): gathered_z[:3]]
  transfers between devices with their start and end apart: 2 -> 0, of which waited for: 2 -> 0; matrix products, arithmetic and copies ran while one was open for 5% -> 0% of each run, Pallas kernels for 0% -> 0%
where the time goes in v3:
time: 82.4 us; the launch traced here: 82.3 us
  Pallas kernels  81.2 us (99%)
  local copies, waits for them, and re-layouts  1.15 us (1%)
    pallas_call x1, Pallas kernels, on_device(): pl.pallas_call(functools.partial(kernel, wide_size, narrow_size), out_sha...  81.2 us

profile of v3, /device:TPU:1, one launch (start us, length us, event | category | flops | bytes accessed | tf_op | source)
XLA Modules:
  0.0 82.3 jit_solution(9491516026770544455)
XLA Ops:
  0.0 81.2 %shard_map.73 = f32[3,32,8,512]{3,2,1,0:T(8,128)S(1)} custom-call(f32[3,32,8,512]{3,2,1,0:T(8,128)} %vel.1, f32[512,512]{1,0:T(8,128)} %sx.1, f32[512,512]{1,0:T(8,128)} %cx.1, f32[256,256]{1,0:T(8,128)} %sy.1, f32[256,256]{1,0:T(8,128)} %cy.1, f32[256,256]{1,0:T(8,128)} %sz.1, f32[256,256]{1,0:T(8,128)} %cz.1), custom_call_target="tpu_custom_call" | custom-call | tf_op jit(solution)/shard_map/pallas_call | solution.py:289
  81.2 1.1 %copy.9 = f32[3,32,8,512]{3,2,1,0:T(8,128)} copy(f32[3,32,8,512]{3,2,1,0:T(8,128)S(1)} %shard_map.73) | data formatting | bytes 3145728

commit v4 on v3

--- a/solution.py
+++ b/solution.py
@@ -68,11 +68,8 @@
 
     barrier = pltpu.get_barrier_semaphore()
 
-    def greet(k, carry):
+    for k in range(group - 1):
         pl.semaphore_signal(barrier, inc=1, device_id=to_place(z_peer(k)), device_id_type=MESH)
-        return carry
-
-    lax.fori_loop(0, group - 1, greet, 0)
     for k in range(1, across):
         pl.semaphore_signal(barrier, inc=1, device_id=to_x((x + k) % across), device_id_type=MESH)
     pl.semaphore_signal(barrier, inc=1, device_id=p_device, device_id_type=MESH)
@@ -105,17 +102,20 @@
 
         lax.fori_loop(0, group - 1, step, 0)
 
-    def send_p(c):
-        send(vel.at[c, :, :, give], pin.at[c], 0, pin_sem.at[c], p_device)
-
-    def send_q(c):
-        send(vel.at[c, :, :, keep], qin.at[c], 1, qin_sem.at[c], q_device)
-
-    def send_z_own(c):
-        def one(to):
+    def send_out(c, q_c):
+        def pieces(k):
+            part = block(k, line_rows)
+            send(vel.at[c, part, :, give], pin.at[c, part], 0, pin_sem.at[c], p_device)
+            send(vel.at[q_c, part, :, keep], qin.at[q_c, part], 1, qin_sem.at[q_c], q_device)
+
+        def step(k, carry):
+            to = z_peer(k)
             send(vel.at[c, block(to, line_rows), :, keep], zin.at[c, :, block(wide, cols)], 2, zin_sem.at[c], to_place(to))
-
-        each_place(one)
+            pieces(k)
+            return carry
+
+        lax.fori_loop(0, group - 1, step, 0)
+        pieces(group - 1)
 
     def send_z_p(c):
         def one(to):
@@ -159,15 +159,17 @@
         arrived(zin.at[c, :, pl.ds(0, 2 * (group - 1) * cols)], zin_sem.at[c])
         line_part(zin, zres, 2, 2, c, line_rows)
 
-        def one_p(to):
+        def one(to):
             send(zres.at[c, :, block((1 - y_lo) * group + to, cols)], zret_p.at[c, block(place, line_rows)], 4, zret_p_sem.at[c], to_place(to))
 
-        def one_o(to):
+        each_place(one)
+        zret_p[c, block(place, line_rows)] = zres[c, :, block(p_wide, cols)]
+
+    def return_own(c):
+        def one(to):
             send(zres.at[c, :, block(y_lo * group + to, cols)], zret_o.at[c, block(place, line_rows)], 4, zret_o_sem.at[c], to_place(to))
 
-        each_place(one_p)
-        each_place(one_o)
-        zret_p[c, block(place, line_rows)] = zres[c, :, block(p_wide, cols)]
+        each_place(one)
         zret_o[c, block(place, line_rows)] = zres[c, :, block(wide, cols)]
 
     def y_part(c):
@@ -209,15 +211,9 @@
         arrived(zret_o.at[c, pl.ds(0, (group - 1) * line_rows)], zret_o_sem.at[c])
         acc[c, :, :, keep] = acc[c, :, :, keep] + zret_o[c]
 
-    send_p(2)
-    send_z_own(2)
-    send_q(1)
-    send_p(1)
-    send_z_own(1)
-    send_q(2)
-    send_p(0)
-    send_z_own(0)
-    send_q(0)
+    send_out(2, 1)
+    send_out(1, 2)
+    send_out(0, 0)
 
     load_vel.wait()
     for c in range(3):
@@ -249,6 +245,7 @@
     x_part(0)
 
     z_part(2)
+    return_own(2)
     y_part(1)
     y_part(2)
     back_to_q(1)
@@ -256,22 +253,24 @@
     y_part(0)
     back_to_q(2)
     z_part(0)
+    return_own(1)
     back_to_q(0)
     back_to_p(2)
     add_q(1)
     add_q(2)
     back_to_p(1)
     add_q(0)
+    back_to_p(0)
+    return_own(0)
     add_p(2)
     add_own(2)
-    back_to_p(0)
     add_p(1)
     add_own(1)
     add_p(0)
     add_own(0)
 
-    parts = [pin, qin, zin.at[:, :, pl.ds(0, 2 * (group - 1) * cols)]] * 2
-    for k, part in ((0, pin), (1, qin), (2, parts[2]), (4, parts[2]), (6, back_q), (7, back_p)):
+    z_blocks = zin.at[:, :, pl.ds(0, 2 * (group - 1) * cols)]
+    for k, part in ((0, pin), (1, qin), (2, z_blocks), (4, z_blocks), (6, back_q), (7, back_p)):
         arrived(part, send_sem.at[k])
     if across > 1:
         for k in (3, 5):

time: 82.4 us -> 79.6 us (0.966)
  Pallas kernels: 81.2 us -> 78.3 us
    pallas_call x1, Pallas kernels: 81.2 us -> 78.3 us  [on_device(): pl.pallas_call(functools.partial(kernel, wide_size, narrow_size), out_sha...]
where the time goes in v4:
time: 79.6 us; the launch traced here: 79.5 us
  Pallas kernels  78.3 us (98%)
  local copies, waits for them, and re-layouts  1.15 us (1%)
    pallas_call x1, Pallas kernels, on_device(): pl.pallas_call(functools.partial(kernel, wide_size, narrow_size), out_sha...  78.3 us

profile of v4, /device:TPU:1, one launch (start us, length us, event | category | flops | bytes accessed | tf_op | source)
XLA Modules:
  0.0 79.5 jit_solution(13348626840696942998)
XLA Ops:
  0.0 78.3 %shard_map.73 = f32[3,32,8,512]{3,2,1,0:T(8,128)S(1)} custom-call(f32[3,32,8,512]{3,2,1,0:T(8,128)} %vel.1, f32[512,512]{1,0:T(8,128)} %sx.1, f32[512,512]{1,0:T(8,128)} %cx.1, f32[256,256]{1,0:T(8,128)} %sy.1, f32[256,256]{1,0:T(8,128)} %cy.1, f32[256,256]{1,0:T(8,128)} %sz.1, f32[256,256]{1,0:T(8,128)} %cz.1), custom_call_target="tpu_custom_call" | custom-call | tf_op jit(solution)/shard_map/pallas_call | solution.py:288
  78.3 1.1 %copy.9 = f32[3,32,8,512]{3,2,1,0:T(8,128)} copy(f32[3,32,8,512]{3,2,1,0:T(8,128)S(1)} %shard_map.73) | data formatting | bytes 3145728

commit v5 on v4

--- a/solution.py
+++ b/solution.py
@@ -165,6 +165,18 @@
         each_place(one)
         zret_p[c, block(place, line_rows)] = zres[c, :, block(p_wide, cols)]
 
+    def return_own_low_first(c, first, count):
+        def step(j, carry):
+            to = (j // deep * (deep // 2) + (z + j % deep // 2) % (deep // 2)) * 2 + (core + 1 - j % 2) % 2
+
+            @pl.when(to != place)
+            def _():
+                send(zres.at[c, :, block(y_lo * group + to, cols)], zret_o.at[c, block(place, line_rows)], 4, zret_o_sem.at[c], to_place(to))
+
+            return carry
+
+        lax.fori_loop(first, first + count, step, 0)
+
     def return_own(c):
         def one(to):
             send(zres.at[c, :, block(y_lo * group + to, cols)], zret_o.at[c, block(place, line_rows)], 4, zret_o_sem.at[c], to_place(to))
@@ -261,7 +273,8 @@
     back_to_p(1)
     add_q(0)
     back_to_p(0)
-    return_own(0)
+    return_own_low_first(0, 0, group)
+    zret_o[0, block(place, line_rows)] = zres[0, :, block(wide, cols)]
     add_p(2)
     add_own(2)
     add_p(1)

time: 79.6 us -> 77.9 us (0.979)
  Pallas kernels: 78.3 us -> 76.7 us
    pallas_call x1, Pallas kernels: 78.3 us -> 76.7 us  [on_device(): pl.pallas_call(functools.partial(kernel, wide_size, narrow_size), out_sha...]
where the time goes in v5:
time: 77.9 us; the launch traced here: 77.8 us
  Pallas kernels  76.7 us (98%)
  local copies, waits for them, and re-layouts  1.15 us (1%)
    pallas_call x1, Pallas kernels, on_device(): pl.pallas_call(functools.partial(kernel, wide_size, narrow_size), out_sha...  76.7 us

profile of v5, /device:TPU:1, one launch (start us, length us, event | category | flops | bytes accessed | tf_op | source)
XLA Modules:
  0.0 77.8 jit_solution(12476318097502438293)
XLA Ops:
  0.0 76.7 %shard_map.73 = f32[3,32,8,512]{3,2,1,0:T(8,128)S(1)} custom-call(f32[3,32,8,512]{3,2,1,0:T(8,128)} %vel.1, f32[512,512]{1,0:T(8,128)} %sx.1, f32[512,512]{1,0:T(8,128)} %cx.1, f32[256,256]{1,0:T(8,128)} %sy.1, f32[256,256]{1,0:T(8,128)} %cy.1, f32[256,256]{1,0:T(8,128)} %sz.1, f32[256,256]{1,0:T(8,128)} %cz.1), custom_call_target="tpu_custom_call" | custom-call | tf_op jit(solution)/shard_map/pallas_call | solution.py:301
  76.7 1.1 %copy.9 = f32[3,32,8,512]{3,2,1,0:T(8,128)} copy(f32[3,32,8,512]{3,2,1,0:T(8,128)S(1)} %shard_map.73) | data formatting | bytes 3145728

commit v6 on v5

--- a/solution.py
+++ b/solution.py
@@ -35,7 +35,7 @@
     pin, qin, ysp, ysq, zin, yin, zres, yres,
     zret_p, zret_o, yret_p, yret_q, psum, back_p, back_q,
     load_sem, send_sem, pin_sem, qin_sem, zin_sem, yin_sem,
-    zret_p_sem, zret_o_sem, yret_p_sem, yret_q_sem, back_p_sem, back_q_sem,
+    zret_p_sem, zret_o_sem, yret_p_sem, yret_q_sem, back_p_sem, back_q_sem, half_sem,
 ):
     wide = lax.axis_index("wide")
     narrow = lax.axis_index("narrow")
@@ -160,7 +160,9 @@
         line_part(zin, zres, 2, 2, c, line_rows)
 
         def one(to):
-            send(zres.at[c, :, block((1 - y_lo) * group + to, cols)], zret_p.at[c, block(place, line_rows)], 4, zret_p_sem.at[c], to_place(to))
+            apart = to // deep - place // deep
+            landed = half_sem.at[apart * apart] if c == 0 else zret_p_sem.at[c]
+            send(zres.at[c, :, block((1 - y_lo) * group + to, cols)], zret_p.at[c, block(place, line_rows)], 4, landed, to_place(to))
 
         each_place(one)
         zret_p[c, block(place, line_rows)] = zres[c, :, block(p_wide, cols)]
@@ -209,6 +211,17 @@
         for plane in range(cols):
             psum[c, :, plane, :] = zret_p[c, :, plane, :] + yret_p[c, plane]
         send(psum.at[c], back_p.at[c], 7, back_p_sem.at[c], p_device)
+
+    def back_to_p_in_halves(c):
+        if across > 1:
+            arrived(yret_p.at[c, pl.ds(0, (across - 1) * planes)], yret_p_sem.at[c])
+        count = deep * line_rows
+        for sem, index, senders in ((1, 1 - place // deep, deep), (0, place // deep, deep - 1)):
+            arrived(zret_p.at[c, pl.ds(0, senders * line_rows)], half_sem.at[sem])
+            part = block(index, count)
+            for plane in range(cols):
+                psum[c, part, plane, :] = zret_p[c, part, plane, :] + yret_p[c, plane, part, :]
+            send(psum.at[c, part], back_p.at[c, part], 7, back_p_sem.at[c], p_device)
 
     def add_q(c):
         arrived(back_q.at[c], back_q_sem.at[c])
@@ -272,7 +285,7 @@
     add_q(2)
     back_to_p(1)
     add_q(0)
-    back_to_p(0)
+    back_to_p_in_halves(0)
     return_own_low_first(0, 0, group)
     zret_o[0, block(place, line_rows)] = zres[0, :, block(wide, cols)]
     add_p(2)
@@ -316,6 +329,7 @@
             dma((7,)),
             dma((8,)),
             *[dma((3,))] * 10,
+            dma((2,)),
         ],
         compiler_params=pltpu.CompilerParams(
             collective_id=0, has_side_effects=True, vmem_limit_bytes=40 * 1024 * 1024

time: 77.9 us -> 77.9 us (level)
  no operation moved by 1% of the time
where the time goes in v6:
time: 77.9 us
  Pallas kernels  76.7 us (98%)
  local copies, waits for them, and re-layouts  1.15 us (1%)
    pallas_call x1, Pallas kernels, on_device(): pl.pallas_call(functools.partial(kernel, wide_size, narrow_size), out_sha...  76.7 us

profile of v6, /device:TPU:1, one launch (start us, length us, event | category | flops | bytes accessed | tf_op | source)
XLA Modules:
  0.0 77.9 jit_solution(15707911696231777970)
XLA Ops:
  0.0 76.7 %shard_map.73 = f32[3,32,8,512]{3,2,1,0:T(8,128)S(1)} custom-call(f32[3,32,8,512]{3,2,1,0:T(8,128)} %vel.1, f32[512,512]{1,0:T(8,128)} %sx.1, f32[512,512]{1,0:T(8,128)} %cx.1, f32[256,256]{1,0:T(8,128)} %sy.1, f32[256,256]{1,0:T(8,128)} %cy.1, f32[256,256]{1,0:T(8,128)} %sz.1, f32[256,256]{1,0:T(8,128)} %cz.1), custom_call_target="tpu_custom_call" | custom-call | tf_op jit(solution)/shard_map/pallas_call | solution.py:314
  76.7 1.1 %copy.9 = f32[3,32,8,512]{3,2,1,0:T(8,128)} copy(f32[3,32,8,512]{3,2,1,0:T(8,128)S(1)} %shard_map.73) | data formatting | bytes 3145728
